TPU v7x, 256 devices: a whole 4x4x8 slice. The times are simulated.
256 devices in a mesh: ea: 128 (over y, z, x), ta: 2 (over core).
Axes of the slice: x: 4, y: 4, z: 8, core: 2. Of those that a mesh axis runs over, the one named last changes fastest.
Arguments:
- sample_inphase: float32 [128, 256, 256], P('ea'), may hold values from 0.2 to 1.2
- sample_quadrature: float32 [128, 256, 256], P('ea'), may hold values from -3 to 3
- beam_inphase: float32 [128, 3, 32, 32], P('ea'), may hold values from -3 to 3
- beam_quadrature: float32 [128, 3, 32, 32], P('ea'), may hold values from -3 to 3
- recorded_diffraction: float32 [128, 2, 16, 32, 32], P('ea', 'ta'), may hold values from 0.05 to 4
- window_corners: int32 [128, 2, 16, 2], P('ea', 'ta'), may hold values from 0 to 224
- filled_tallies: int32 [128, 2], P('ea', 'ta'), may hold values from 1 to 16, 24 in all within a row
- absorption_templates: float32 [16, 128], replicated, may hold values from -6 to 6
Outputs:
- fitted: float32 [2, 128, 128, 2, 256], P(None, 'ea', None, 'ta')
- coefficients: float32 [2, 16, 65536], P(None, None, ('ea', 'ta'))
Inputs may be any that keep to these rules, and one draw needn't show every extreme that they name: `filled_tallies`: in each energy the two tiles' counts sum to 24 and the larger is at most 16. `window_corners`: offsets of slots at or past their tile's count are not used.
All inputs are finite; a program needn't handle non-finite values. No bound on the sum of `filled_tallies` on one device may be relied on, other than what follows from the above.
Results may differ from a plain program's by a relative error of at most 0.0003.
Values sent between devices are 32-bit elements; how exact they have to be, the bound alone decides.
A program may use at most 64 MiB of HBM per device.

v0:
```python
import jax
import jax.numpy as jnp
from jax import lax
from jax.sharding import PartitionSpec as P

HIGHEST_PRECISION = lax.Precision.HIGHEST
FLOOR_POWER = 0.5
REGULARIZER = 1.0


def dft_tables(length):
    counter = jnp.arange(length, dtype=jnp.int32)
    product = counter[:, None] * counter[None, :] % length
    angles = 2.0 * jnp.pi / length * product.astype(jnp.float32)
    norming = 1.0 / jnp.sqrt(jnp.float32(length))
    return (jnp.cos(angles) * norming, -jnp.sin(angles) * norming)


def two_sided(field_re, field_im, table_re, table_im):
    left_re = jnp.einsum(
        "jk,...kl->...jl", table_re, field_re, precision=HIGHEST_PRECISION
    ) - jnp.einsum("jk,...kl->...jl", table_im, field_im, precision=HIGHEST_PRECISION)
    left_im = jnp.einsum(
        "jk,...kl->...jl", table_re, field_im, precision=HIGHEST_PRECISION
    ) + jnp.einsum("jk,...kl->...jl", table_im, field_re, precision=HIGHEST_PRECISION)
    right_re = jnp.einsum(
        "...jk,kl->...jl", left_re, table_re, precision=HIGHEST_PRECISION
    ) - jnp.einsum("...jk,kl->...jl", left_im, table_im, precision=HIGHEST_PRECISION)
    right_im = jnp.einsum(
        "...jk,kl->...jl", left_re, table_im, precision=HIGHEST_PRECISION
    ) + jnp.einsum("...jk,kl->...jl", left_im, table_re, precision=HIGHEST_PRECISION)
    return (right_re, right_im)


def slot_terms(
    sample_inphase,
    sample_quadrature,
    beam_inphase,
    beam_quadrature,
    intensity,
    corners,
    weight,
    table_re,
    table_im,
):
    width = beam_inphase.shape[-1]

    def extract(source, corner):
        return lax.dynamic_slice(source, (corner[0], corner[1]), (width, width))

    patch_re = jax.vmap(extract, (None, 0))(sample_inphase, corners)
    patch_im = jax.vmap(extract, (None, 0))(sample_quadrature, corners)
    exit_re = beam_inphase[None] * patch_re[:, None] - beam_quadrature[None] * patch_im[:, None]
    exit_im = beam_inphase[None] * patch_im[:, None] + beam_quadrature[None] * patch_re[:, None]
    far_re, far_im = two_sided(exit_re, exit_im, table_re, table_im)
    power = jnp.sum(far_re * far_re + far_im * far_im, axis=1)
    factor = (1.0 - jnp.sqrt(intensity) / jnp.sqrt(jnp.maximum(power, FLOOR_POWER))) * weight[
        :, None, None
    ]
    back_re, back_im = two_sided(
        far_re * factor[:, None], far_im * factor[:, None], table_re, -table_im
    )
    terms_re = jnp.sum(beam_inphase[None] * back_re + beam_quadrature[None] * back_im, axis=1)
    terms_im = jnp.sum(beam_inphase[None] * back_im - beam_quadrature[None] * back_re, axis=1)
    return (terms_re, terms_im)


def deposit(field, patch, corner):
    width = patch.shape[0]
    current = lax.dynamic_slice(field, (corner[0], corner[1]), (width, width))
    return lax.dynamic_update_slice(field, current + patch, (corner[0], corner[1]))


def local(
    sample_inphase,
    sample_quadrature,
    beam_inphase,
    beam_quadrature,
    recorded_diffraction,
    window_corners,
    filled_tallies,
    absorption_templates,
):
    local_energies = sample_inphase.shape[0]
    side = sample_inphase.shape[1]
    spot_numbering = recorded_diffraction.shape[2]
    width = beam_inphase.shape[-1]
    blocks = lax.axis_size("ea")
    tiles = lax.axis_size("ta")
    tile = lax.axis_index("ta")
    table_re, table_im = dft_tables(width)
    group = 8
    first_slot = jnp.zeros((local_energies,), jnp.int32)
    taken_slots = filled_tallies[:, 0]
    tile_boundary = jnp.full((local_energies,), spot_numbering, jnp.int32)
    gathered_recordings = recorded_diffraction[:, 0]
    pooled_offsets = window_corners[:, 0]

    def lone_wavelength(items):
        o_re, o_im, p_re, p_im, intensity_pool, corner_pool, start, number, split = items
        light_patch = jnp.sum(p_re * p_re + p_im * p_im, axis=0)
        zeros = jnp.zeros((side, side), jnp.float32)

        def advance(index, carry):
            grad_re, grad_im, light = carry
            position = start + index * group + jnp.arange(group, dtype=jnp.int32)
            weight = (position < start + number).astype(jnp.float32)
            source = jnp.where(position < split, position, spot_numbering + position - split)
            source = jnp.clip(source, 0, intensity_pool.shape[0] - 1)
            corners = corner_pool[source]
            terms_re, terms_im = slot_terms(
                o_re, o_im, p_re, p_im, intensity_pool[source], corners, weight, table_re, table_im
            )
            for member in range(group):
                grad_re = deposit(grad_re, terms_re[member], corners[member])
                grad_im = deposit(grad_im, terms_im[member], corners[member])
                light = deposit(light, light_patch * weight[member], corners[member])
            return (grad_re, grad_im, light)

        rounds = (number + group - 1) // group
        return lax.fori_loop(0, rounds, advance, (zeros, zeros, zeros))

    grad_re, grad_im, light = lax.map(
        lone_wavelength,
        (
            sample_inphase,
            sample_quadrature,
            beam_inphase,
            beam_quadrature,
            gathered_recordings,
            pooled_offsets,
            first_slot,
            taken_slots,
            tile_boundary,
        ),
    )

    def shares(field):
        return field.reshape(local_energies, blocks, tiles, -1)

    summed = lax.psum_scatter(
        jnp.stack([shares(grad_re), shares(grad_im), shares(light)]),
        "ta",
        scatter_dimension=3,
        tiled=True,
    )
    light_share = summed[2]
    own_re = lax.dynamic_slice_in_dim(shares(sample_inphase), tile, 1, 2)
    own_im = lax.dynamic_slice_in_dim(shares(sample_quadrature), tile, 1, 2)
    revised_inphase = own_re - summed[0] / (light_share + REGULARIZER)
    revised_quadrature = own_im - summed[1] / (light_share + REGULARIZER)
    spectra = jnp.stack([revised_inphase, revised_quadrature])[:, :, :, 0, :]
    gram = jnp.dot(absorption_templates, absorption_templates.T, precision=HIGHEST_PRECISION)
    factor_low = jnp.linalg.cholesky(gram)
    project = jax.scipy.linalg.cho_solve((factor_low, True), absorption_templates)
    values = lax.all_to_all(spectra, "ea", split_axis=2, concat_axis=1, tiled=True)[:, :, 0, :]
    coefs = jnp.einsum("ke,cen->ckn", project, values, precision=HIGHEST_PRECISION)
    fitted_here = jnp.einsum(
        "ke,ckn->cen", absorption_templates, coefs, precision=HIGHEST_PRECISION
    )
    returned = lax.all_to_all(
        fitted_here[:, :, None, :], "ea", split_axis=1, concat_axis=2, tiled=True
    )
    coef_local = coefs[:, :, None, :]
    return (returned[:, :, :, None, :], coef_local[:, :, 0, :])


def solution(mesh):
    in_specs = (
        P("ea", None, None),
        P("ea", None, None),
        P("ea", None, None, None),
        P("ea", None, None, None),
        P("ea", "ta", None, None, None),
        P("ea", "ta", None, None),
        P("ea", "ta"),
        P(),
    )
    out_specs = (P(None, "ea", None, "ta", None), P(None, None, ("ea", "ta")))
    return jax.shard_map(local, mesh=mesh, in_specs=in_specs, out_specs=out_specs, check_vma=False)
```

profile of v0, /device:TPU:1, one launch (start us, length us, event | category | flops | bytes accessed | tf_op | source)
XLA Modules:
  0.0 321.4 jit_solution(4731289166006635438)
XLA Ops:
  10.6 215.1 %while.42 = (s32[]{:T(128)}, f32[256,256]{1,0:T(8,128)S(1)}, f32[256,256]{1,0:T(8,128)S(1)}, f32[256,256]{1,0:T(8,128)S(1)}, s32[]{:T(128)}, /*index=5*/s32[16,2...) while((s32[]{:T(128)}, f32[256,256]{1,0:T(8,128)S(1)}, ...), condition=%wide.region_5.6_spmd.clone.clone, body=%wide.region_1.5_spmd.clone.clone.sunk | while | flops 152179840 | bytes 5044471 | solution.py:121
  23.5 1.1 dynamic_update_slice.336
  29.1 1.1 dynamic_update_slice.337
  57.0 14.9 %while.44 = (s32[]{:T(128)}, f32[256,256]{1,0:T(8,128)S(1)}, s32[8,2]{0,1:T(2,128)S(1)}, f32[8,32,32]{2,1,0:T(8,128)S(1)}, s32[]{:T(128)}) while((s32[]{:T(128)}, f32[256,256]{1,0:T(8,128)S(1)}, s32[8,2]{0,1:T(2,128)S(1)}, f32[8,32,32]{2,1,0:T(8,128)S(1)}, s32[]{:T(128)}) %tuple.143), condition=%wide.while_cond, body=%wide.while_body.sunk | while | flops 2 | bytes 32877 | solution.py:49
  57.6 1.3 bitcast_dynamic-update-slice_fusion.5
  59.5 1.3 bitcast_dynamic-update-slice_fusion.5
  61.3 1.3 bitcast_dynamic-update-slice_fusion.5
  63.2 1.3 bitcast_dynamic-update-slice_fusion.5
  65.0 1.3 bitcast_dynamic-update-slice_fusion.5
  66.9 1.3 bitcast_dynamic-update-slice_fusion.5
  68.8 1.3 bitcast_dynamic-update-slice_fusion.5
  70.6 1.3 bitcast_dynamic-update-slice_fusion.5
  71.9 14.9 %while.43 = (s32[]{:T(128)}, f32[256,256]{1,0:T(8,128)S(1)}, s32[8,2]{0,1:T(2,128)S(1)}, f32[8,32,32]{2,1,0:T(8,128)S(1)}, s32[]{:T(128)}) while((s32[]{:T(128)}, f32[256,256]{1,0:T(8,128)S(1)}, s32[8,2]{0,1:T(2,128)S(1)}, f32[8,32,32]{2,1,0:T(8,128)S(1)}, s32[]{:T(128)}) %tuple.153), condition=%wide.while_cond.1, body=%wide.while_body.1.sunk | while | flops 2 | bytes 32877 | solution.py:49
  72.5 1.3 bitcast_dynamic-update-slice_fusion.4
  74.4 1.3 bitcast_dynamic-update-slice_fusion.4
  76.2 1.3 bitcast_dynamic-update-slice_fusion.4
  78.1 1.3 bitcast_dynamic-update-slice_fusion.4
  80.0 1.3 bitcast_dynamic-update-slice_fusion.4
  81.8 1.3 bitcast_dynamic-update-slice_fusion.4
  83.7 1.3 bitcast_dynamic-update-slice_fusion.4
  85.5 1.3 bitcast_dynamic-update-slice_fusion.4
  100.5 1.1 dynamic_update_slice.327
  101.7 1.1 dynamic_update_slice.328
  102.9 1.1 dynamic_update_slice.329
  108.8 1.1 dynamic_update_slice.319
  110.0 1.1 dynamic_update_slice.320
  111.2 1.1 dynamic_update_slice.321
  124.7 1.1 dynamic_update_slice.335
  135.4 1.1 dynamic_update_slice.337
  157.4 1.1 dynamic_update_slice.341
  164.1 14.9 %while.44 = (s32[]{:T(128)}, f32[256,256]{1,0:T(8,128)S(1)}, s32[8,2]{0,1:T(2,128)S(1)}, f32[8,32,32]{2,1,0:T(8,128)S(1)}, s32[]{:T(128)}) while((s32[]{:T(128)}, f32[256,256]{1,0:T(8,128)S(1)}, s32[8,2]{0,1:T(2,128)S(1)}, f32[8,32,32]{2,1,0:T(8,128)S(1)}, s32[]{:T(128)}) %tuple.143), condition=%wide.while_cond, body=%wide.while_body.sunk | while | flops 2 | bytes 32877 | solution.py:49
  164.8 1.3 bitcast_dynamic-update-slice_fusion.5
  166.6 1.3 bitcast_dynamic-update-slice_fusion.5
  168.5 1.3 bitcast_dynamic-update-slice_fusion.5
  170.3 1.3 bitcast_dynamic-update-slice_fusion.5
  172.2 1.3 bitcast_dynamic-update-slice_fusion.5
  174.1 1.3 bitcast_dynamic-update-slice_fusion.5
  175.9 1.3 bitcast_dynamic-update-slice_fusion.5
  177.8 1.3 bitcast_dynamic-update-slice_fusion.5
  179.1 14.9 %while.43 = (s32[]{:T(128)}, f32[256,256]{1,0:T(8,128)S(1)}, s32[8,2]{0,1:T(2,128)S(1)}, f32[8,32,32]{2,1,0:T(8,128)S(1)}, s32[]{:T(128)}) while((s32[]{:T(128)}, f32[256,256]{1,0:T(8,128)S(1)}, s32[8,2]{0,1:T(2,128)S(1)}, f32[8,32,32]{2,1,0:T(8,128)S(1)}, s32[]{:T(128)}) %tuple.153), condition=%wide.while_cond.1, body=%wide.while_body.1.sunk | while | flops 2 | bytes 32877 | solution.py:49
  179.7 1.3 bitcast_dynamic-update-slice_fusion.4
  181.5 1.3 bitcast_dynamic-update-slice_fusion.4
  183.4 1.3 bitcast_dynamic-update-slice_fusion.4
  185.3 1.3 bitcast_dynamic-update-slice_fusion.4
  187.1 1.3 bitcast_dynamic-update-slice_fusion.4
  189.0 1.3 bitcast_dynamic-update-slice_fusion.4
  190.8 1.3 bitcast_dynamic-update-slice_fusion.4
  192.7 1.3 bitcast_dynamic-update-slice_fusion.4
  207.7 1.1 dynamic_update_slice.327
  209.8 1.1 dynamic_update_slice.329
  214.3 1.1 dynamic_update_slice.333
  215.5 1.1 dynamic_update_slice.334
  216.6 1.1 dynamic_update_slice.319
  220.9 1.1 dynamic_update_slice.323
  222.1 1.1 dynamic_update_slice.324
  223.3 1.1 dynamic_update_slice.325
  224.5 1.1 dynamic_update_slice.326
  228.3 1.5 cholesky.16
  231.7 32.5 %all-reduce.3.cloned.1.call-done = f32[3,1,128,2,256]{4,2,3,1,0:T(8,128)} async-done(((f32[3,1,128,2,256]{4,2,3,1,0:T(8,128)}), f32[3,1,128,2,256]{4,2,3,1,0:T(8,128)}) %all-reduce.3.cloned.1.call-update) | async-done | bytes 786448
  264.2 1.7 constant_dynamic-slice_fusion.3
  267.3 13.6 %all-to-all-start = ((f32[2,1,128,256]{3,0,1,2:T(2,128)}), f32[2,1,128,256]{3,0,1,2:T(2,128)S(1)}, u32[]{:S(2)}, u32[]{:S(2)}) async-start(f32[2,1,128,256]{3,0,1,2:T(2,128)} %maximum_bitcast_fusion), calls=%async_computation | async-start | bytes 524288 | tf_op jit(solution)/shard_map/all_to_all | solution.py:156
  281.5 1.2 custom-call.10
  283.1 10.9 %all-to-all-done = f32[2,1,128,256]{3,0,1,2:T(2,128)S(1)} async-done(((f32[2,1,128,256]{3,0,1,2:T(2,128)}), f32[2,1,128,256]{3,0,1,2:T(2,128)S(1)}, u32[]{:S(2)}, u32[]{:S(2)}) %all-to-all-start) | async-done | bytes 262176 | tf_op jit(solution)/shard_map/all_to_all | solution.py:156
  295.1 18.6 %all_to_all.8 = f32[2,128,1,256]{3,0,2,1:T(2,128)S(1)} all-to-all(f32[2,128,1,256]{3,0,2,1:T(2,128)S(1)} %copy.85), channel_id=1, replica_groups=mesh['ea'=128,'ta'=2] {'ea'}, dimensions={1} | all-to-all | bytes 524288 | tf_op jit(solution)/shard_map/all_to_all | solution.py:161
  (245 shorter events, 103.7 us)
Async XLA Ops:
  7.2 221.0 %copy-start = (f32[16,128]{1,0:T(8,128)S(1)}, f32[16,128]{1,0:T(8,128)}, u32[]{:S(2)}) copy-start(f32[16,128]{1,0:T(8,128)} %param.17) | copy-start | bytes 24580
  7.2 257.0 %all-reduce.3.cloned.1.call-start = ((), (), s32[]{:S(2)}) async-start(), calls=%async_computation.2 | async-start | bytes 1572864
  7.9 0.7 copy-start.7
  8.7 1.0 copy-start.5
  9.5 1.0 copy-start.4
  9.6 1.0 copy-start.3
  9.6 1.0 copy-start.1
  9.6 1.0 copy-start.2
  229.8 0.7 copy-start.8
  267.3 26.7 %all-to-all-start = ((f32[2,1,128,256]{3,0,1,2:T(2,128)}), f32[2,1,128,256]{3,0,1,2:T(2,128)S(1)}, u32[]{:S(2)}, u32[]{:S(2)}) async-start(f32[2,1,128,256]{3,0,1,2:T(2,128)} %maximum_bitcast_fusion), calls=%async_computation | async-start | bytes 524288 | tf_op jit(solution)/shard_map/all_to_all | solution.py:156
  294.3 0.6 copy-start.6
Sparse Core Ops, SparseCore 0:
  227.7 36.4 all-reduce.2
where the time goes:
time: 325 us; the launch traced here: 321 us
  local copies, waits for them, and re-layouts  120 us (37%)
  loops' own time  60.9 us (19%)
  waiting for transfers between devices  43.4 us (13%)
  matrix products  27 us (8%)
  other arithmetic  22.7 us (7%)
  blocking collectives  18.6 us (6%)
  between operations  14.9 us (5%)
  starting transfers between devices  13.6 us (4%)
    another operation x1, loops' own time, lone_wavelength(): return lax.fori_loop(0, rounds, advance, (zeros, zeros, zeros))  60.8 us
    gather x96, local copies, waits for them, and re-layouts  59.5 us
    dynamic_update_slice x48, local copies, waits for them, and re-layouts, deposit(): lax.dynamic_update_slice(field, current + patch, (corner[0], corner[1]))  47.6 us
    unnamed x2, waiting for transfers between devices  32.5 us
    all_to_all x1, blocking collectives, local(): lax.all_to_all(fitted_here[:, :, None, :], 'ea', split_axis=1, concat_axi...  18.6 us
    add x46, other arithmetic, deposit(): current + patch  14.2 us
    all_to_all x1, starting transfers between devices, local(): lax.all_to_all(spectra, 'ea', split_axis=2, concat_axis=1, tiled=True)  13.6 us
    all_to_all x1, waiting for transfers between devices, local(): lax.all_to_all(spectra, 'ea', split_axis=2, concat_axis=1, tiled=True)  10.9 us
  transfers between devices with their start and end apart: 2, of which 2 were waited for; matrix products, arithmetic and copies ran while one was open for 2% of the time, Pallas kernels for 0%

commit v1 on v0

v1 whole, which is shorter than its diff:
```python
import functools

import jax
import jax.numpy as jnp
import numpy as np
from jax import lax
from jax.experimental import pallas as pl
from jax.experimental.pallas import tpu as pltpu
from jax.sharding import PartitionSpec as P

MESH = pl.DeviceIdType.MESH
HIGHEST = lax.Precision.HIGHEST
FLOOR_POWER = 0.5
REGULARIZER = 1.0
ENERGIES = 128
EDGES = 16
SIDE = 256
HALF = 128
WIDTH = 32
MODES = 3
SLOTS = 16
PER_GROUP = 4
GROUPS = SLOTS // PER_GROUP
BAND = MODES * WIDTH
LANES = PER_GROUP * WIDTH
VMEM_BYTES = 48 * 1024 * 1024


def split_table(table):
    high = table.astype(jnp.bfloat16)
    low = (table - high.astype(np.float32)).astype(jnp.bfloat16)
    return np.stack([high, low])


def dft_matrices():
    index = np.arange(WIDTH)
    angles = 2.0 * np.pi / WIDTH * (index[:, None] * index[None, :] % WIDTH)
    re, im = np.cos(angles) / np.sqrt(WIDTH), -np.sin(angles) / np.sqrt(WIDTH)
    tables = []
    for sign in (1.0, -1.0):
        b_re, b_im = (np.kron(np.eye(PER_GROUP), part) for part in (re, sign * im))
        l_re, l_im = (np.kron(np.eye(MODES), part) for part in (re, sign * im))
        right = np.block([[b_re, b_im], [-b_im, b_re]]).astype(np.float32)
        left = np.block([[l_re, -l_im], [l_im, l_re]]).astype(np.float32)
        tables += [split_table(right), split_table(left)]
    return tables


def halves(value):
    high = value.astype(jnp.bfloat16)
    return high, (value - high.astype(jnp.float32)).astype(jnp.bfloat16)


def product(a, b):
    dot = functools.partial(jnp.dot, preferred_element_type=jnp.float32)
    return dot(a[0], b[0]) + (dot(a[0], b[1]) + dot(a[1], b[0]))


def slots_kernel(
    corners,
    tallies,
    o_re,
    o_im,
    p_re,
    p_im,
    intensity,
    right_f,
    left_f,
    right_b,
    left_b,
    out,
    objects,
    totals,
):
    tally = tallies[0, 0]
    for part, source in enumerate((o_re, o_im)):
        for half in range(2):
            lanes = slice(half * HALF, (half + 1) * HALF)
            objects[pl.ds(2 * part + half, SIDE, stride=4), :] = source[0, :, lanes]
    totals[...] = jnp.zeros_like(totals)
    probe_re = [jnp.concatenate([p_re[0, m]] * PER_GROUP, axis=1) for m in range(MODES)]
    probe_im = [jnp.concatenate([p_im[0, m]] * PER_GROUP, axis=1) for m in range(MODES)]
    light = sum(a * a + b * b for a, b in zip(probe_re, probe_im))
    lane = lax.broadcasted_iota(jnp.int32, (WIDTH, LANES), 1)

    bands = []
    for g in range(GROUPS):
        patch = [jnp.zeros((WIDTH, LANES), jnp.float32)] * 2
        for j in range(PER_GROUP):
            s = g * PER_GROUP + j
            row, column = corners[s, 0], corners[s, 1]
            shift = lax.rem(WIDTH * j + SIDE - column, HALF)
            for part in range(2):
                left, right = (objects[pl.ds(4 * row + 2 * part + half, WIDTH, stride=4), :] for half in range(2))
                rolled = pltpu.roll(jnp.where(lane >= column, left, right), shift, 1)
                patch[part] = jnp.where(lane // WIDTH == j, rolled, patch[part])
        exits_re = [a * patch[0] - b * patch[1] for a, b in zip(probe_re, probe_im)]
        exits_im = [a * patch[1] + b * patch[0] for a, b in zip(probe_re, probe_im)]
        bands.append(
            jnp.concatenate(
                [jnp.concatenate(exits_re, axis=0), jnp.concatenate(exits_im, axis=0)], axis=1
            )
        )
    wide = product(halves(jnp.concatenate(bands, axis=0)), (right_f[0], right_f[1]))
    tall = jnp.concatenate(
        [
            jnp.concatenate([wide[g * BAND : (g + 1) * BAND, h * LANES : (h + 1) * LANES] for g in range(GROUPS)], axis=1)
            for h in range(2)
        ],
        axis=0,
    )
    far = product((left_f[0], left_f[1]), halves(tall))
    power = sum(
        far[k * WIDTH : (k + 1) * WIDTH] * far[k * WIDTH : (k + 1) * WIDTH] for k in range(2 * MODES)
    )
    measured = jnp.concatenate([intensity[0, 0, s] for s in range(SLOTS)], axis=1)
    used = lax.broadcasted_iota(jnp.int32, (WIDTH, GROUPS * LANES), 1) // WIDTH < tally
    factor = jnp.where(used, 1.0 - jnp.sqrt(measured) / jnp.sqrt(jnp.maximum(power, FLOOR_POWER)), 0.0)
    corrected = far * jnp.concatenate([factor] * (2 * MODES), axis=0)
    tall = product((left_b[0], left_b[1]), halves(corrected))
    wide = jnp.concatenate(
        [
            jnp.concatenate([tall[h * BAND : (h + 1) * BAND, g * LANES : (g + 1) * LANES] for h in range(2)], axis=1)
            for g in range(GROUPS)
        ],
        axis=0,
    )
    back = product(halves(wide), (right_b[0], right_b[1]))
    for g in range(GROUPS):
        term_re, term_im = jnp.zeros((2, WIDTH, LANES), jnp.float32)
        for m in range(MODES):
            rows = slice(g * BAND + m * WIDTH, g * BAND + (m + 1) * WIDTH)
            b_re, b_im = back[rows, :LANES], back[rows, LANES:]
            term_re += probe_re[m] * b_re + probe_im[m] * b_im
            term_im += probe_re[m] * b_im - probe_im[m] * b_re
        for j in range(PER_GROUP):
            s = g * PER_GROUP + j
            row, column = corners[s, 0], corners[s, 1]
            shift = lax.rem(column + HALF - WIDTH * j, HALF)
            weight = jnp.where(s < tally, 1.0, 0.0)
            for field, term in enumerate((term_re, term_im, light * weight)):
                alone = pltpu.roll(jnp.where(lane // WIDTH == j, term, 0.0), shift, 1)
                for half, part in enumerate((jnp.where(lane >= column, alone, 0.0), jnp.where(lane < column, alone, 0.0))):
                    totals[field, pl.ds(2 * row + half, WIDTH, stride=2), :] += part
    for parity in range(2):
        for half in range(2):
            lanes = slice(half * HALF, (half + 1) * HALF)
            for field in range(3):
                out[parity, field, :, lanes] = totals[field, pl.ds(2 * parity + half, SIDE // 2, stride=4), :]
            for part in range(2):
                out[parity, 3 + part, :, lanes] = objects[pl.ds(4 * parity + 2 * part + half, SIDE // 2, stride=8), :]


def projection(templates):
    gram = lax.dot_general(
        templates, templates, (((1,), (1,)), ((), ())), precision=HIGHEST, preferred_element_type=jnp.float32
    )
    table = jnp.concatenate(
        [gram, jnp.zeros((EDGES, ENERGIES - EDGES), jnp.float32), templates], axis=1
    )
    which = lax.broadcasted_iota(jnp.int32, table.shape, 0)
    for k in range(EDGES):
        pivot = table[k : k + 1, :] / table[k : k + 1, k : k + 1]
        table = jnp.where(which == k, pivot, table - table[:, k : k + 1] * pivot)
    return table[:, ENERGIES:]


def exchange_kernel(
    fields,
    templates_ref,
    fitted,
    coefficients,
    partner,
    spectra,
    values,
    answer,
    landed,
    arrivals,
    sems,
):
    me, core = lax.axis_index("ea"), lax.axis_index("ta")
    barrier = pltpu.get_barrier_semaphore()

    def peer_of(step):
        return lax.rem(me + 1 + step, ENERGIES)

    def greet(step, carry):
        pl.semaphore_signal(barrier, inc=1, device_id={"ea": peer_of(step)}, device_id_type=MESH)
        return carry

    pl.semaphore_signal(barrier, inc=1, device_id={"ta": 1 - core}, device_id_type=MESH)
    lax.fori_loop(0, ENERGIES - 1, greet, 0)
    pl.semaphore_wait(barrier, ENERGIES)

    swap = pltpu.make_async_remote_copy(
        src_ref=fields.at[1 - core, pl.ds(0, 3)],
        dst_ref=partner,
        send_sem=sems.at[0],
        recv_sem=sems.at[1],
        device_id={"ta": 1 - core},
        device_id_type=MESH,
    )
    swap.start()
    swap.wait()
    scale = fields[core, 2] + partner[2] + REGULARIZER
    for part in range(2):
        own = fields[core, 3 + part]
        spectra[:, part * SIDE : (part + 1) * SIDE] = own - (fields[core, part] + partner[part]) / scale

    def send_all(source, target, first):
        def send(step, carry):
            peer = peer_of(step)
            pltpu.make_async_remote_copy(
                src_ref=source.at[pl.ds(peer, 1)],
                dst_ref=target.at[pl.ds(me, 1)],
                send_sem=sems.at[first],
                recv_sem=sems.at[first + 1],
                device_id={"ea": peer},
                device_id_type=MESH,
            ).start()
            return carry

        lax.fori_loop(0, ENERGIES - 1, send, 0)
        target[pl.ds(me, 1), :] = source[pl.ds(me, 1), :]

    def wait_all(first):
        pltpu.make_async_remote_copy(
            src_ref=arrivals,
            dst_ref=arrivals,
            send_sem=sems.at[first],
            recv_sem=sems.at[first + 1],
            device_id={"ea": peer_of(0)},
            device_id_type=MESH,
        ).wait()

    send_all(spectra, values, 2)
    templates = templates_ref[...]
    project = projection(templates)
    wait_all(2)
    coefs = jnp.dot(project, values[...], precision=HIGHEST, preferred_element_type=jnp.float32)
    for part in range(2):
        coefficients[part] = coefs[:, part * SIDE : (part + 1) * SIDE]
    answer[...] = lax.dot_general(
        templates, coefs, (((0,), (0,)), ((), ())), precision=HIGHEST, preferred_element_type=jnp.float32
    )
    send_all(answer, landed, 4)
    wait_all(4)
    for part in range(2):
        fitted[part] = landed[:, part * SIDE : (part + 1) * SIDE]


def local(
    sample_inphase,
    sample_quadrature,
    beam_inphase,
    beam_quadrature,
    recorded_diffraction,
    window_corners,
    filled_tallies,
    absorption_templates,
):
    vmem = pl.BlockSpec(memory_space=pltpu.VMEM)
    smem = pl.BlockSpec(memory_space=pltpu.SMEM)
    fields = pl.pallas_call(
        slots_kernel,
        out_shape=jax.ShapeDtypeStruct((2, 5, SIDE // 2, SIDE), jnp.float32),
        in_specs=[smem, smem] + [vmem] * 9,
        out_specs=vmem,
        scratch_shapes=[
            pltpu.VMEM((4 * SIDE, HALF), jnp.float32),
            pltpu.VMEM((3, 2 * SIDE, HALF), jnp.float32),
        ],
        compiler_params=pltpu.CompilerParams(vmem_limit_bytes=VMEM_BYTES),
    )(
        window_corners[0, 0],
        filled_tallies,
        sample_inphase,
        sample_quadrature,
        beam_inphase,
        beam_quadrature,
        recorded_diffraction,
        *[jnp.asarray(table) for table in dft_matrices()],
    )
    rows = pltpu.VMEM((ENERGIES, 2 * SIDE), jnp.float32)
    fitted, coefficients = pl.pallas_call(
        exchange_kernel,
        out_shape=(
            jax.ShapeDtypeStruct((2, ENERGIES, SIDE), jnp.float32),
            jax.ShapeDtypeStruct((2, EDGES, SIDE), jnp.float32),
        ),
        in_specs=[vmem] * 2,
        out_specs=(vmem, vmem),
        scratch_shapes=[
            pltpu.VMEM((3, SIDE // 2, SIDE), jnp.float32),
            rows,
            rows,
            rows,
            rows,
            pltpu.VMEM((ENERGIES - 1, 1, 2 * SIDE), jnp.float32),
            pltpu.SemaphoreType.DMA((6,)),
        ],
        compiler_params=pltpu.CompilerParams(
            collective_id=0, has_side_effects=True, vmem_limit_bytes=VMEM_BYTES
        ),
    )(fields, absorption_templates)
    return (fitted[:, None, :, None, :], coefficients)


def solution(mesh):
    in_specs = (
        P("ea", None, None),
        P("ea", None, None),
        P("ea", None, None, None),
        P("ea", None, None, None),
        P("ea", "ta", None, None, None),
        P("ea", "ta", None, None),
        P("ea", "ta"),
        P(),
    )
    out_specs = (P(None, "ea", None, "ta", None), P(None, None, ("ea", "ta")))
    return jax.shard_map(local, mesh=mesh, in_specs=in_specs, out_specs=out_specs, check_vma=False)
```

time: 325 us -> 50.6 us (0.16)
  local copies, waits for them, and re-layouts: 120 us -> 10.5 us
  loops' own time: 60.9 us -> 0 us
  waiting for transfers between devices: 43.4 us -> 0 us
  Pallas kernels: 0 us -> 38.3 us
  matrix products: 27 us -> 0 us
  other arithmetic: 22.7 us -> 0 us
  blocking collectives: 18.6 us -> 0 us
  starting transfers between devices: 13.6 us -> 0 us
  between operations: 14.9 us -> 1.31 us
    gather x100 -> x0, local copies, waits for them, and re-layouts: 61.7 us -> none
    another operation x5 -> x0, loops' own time: 60.9 us -> none  [the longest x1 60.8 us: lone_wavelength(): return lax.fori_loop(0, rounds, advance, (zeros, zeros, zeros))]
    dynamic_update_slice x48 -> x0, local copies, waits for them, and re-layouts: 47.6 us -> none  [deposit(): lax.dynamic_update_slice(field, current + patch, (corner[0], corner[1]))]
    pallas_call x0 -> x2, Pallas kernels: none -> 38.3 us  [the longest x1 35.6 us: local(): pl.pallas_call(exchange_kernel, out_shape=(jax.ShapeDtypeStruct((2, ENERG...]
    unnamed x2 -> x0, waiting for transfers between devices: 32.5 us -> none
    dot_general x35 -> x0, matrix products: 26.7 us -> none  [the longest x4 3.25 us: two_sided(): jnp.einsum('jk,...kl->...jl', table_im, field_re, precision=HIGHEST_PRECI...]
    all_to_all x1 -> x0, blocking collectives: 18.6 us -> none  [local(): lax.all_to_all(fitted_here[:, :, None, :], 'ea', split_axis=1, concat_axi...]
    add x46 -> x0, other arithmetic: 14.2 us -> none  [deposit(): current + patch]
  transfers between devices with their start and end apart: 2 -> 0, of which waited for: 2 -> 0; matrix products, arithmetic and copies ran while one was open for 2% -> 0% of each run, Pallas kernels for 0% -> 0%
where the time goes in v1:
time: 50.6 us; the launch traced here: 50.2 us
  Pallas kernels  38.3 us (76%)
  local copies, waits for them, and re-layouts  10.5 us (21%)
  between operations  1.31 us (3%)
    pallas_call x1, Pallas kernels, local(): pl.pallas_call(exchange_kernel, out_shape=(jax.ShapeDtypeStruct((2, ENERG...  35.6 us
    unnamed x22, local copies, waits for them, and re-layouts  9.79 us
    pallas_call x1, Pallas kernels, local(): pl.pallas_call(slots_kernel, out_shape=jax.ShapeDtypeStruct((2, 5, SIDE /...  2.72 us

profile of v1, /device:TPU:1, one launch (start us, length us, event | category | flops | bytes accessed | tf_op | source)
XLA Modules:
  0.0 50.2 jit_solution(12243402239895055147)
XLA Ops:
  1.3 0.8 %copy.14.corners = s32[16,2]{1,0:T(8,128)S(1)} copy(s32[16,2]{0,1:T(2,128)} %bitcast.3) | data formatting | bytes 256 | tf_op jit(solution)/shard_map/squeeze | solution.py:275
  2.0 0.0 copy-start
  2.0 0.9 %copy-done = f32[1,256,256]{2,1,0:T(8,128)S(1)} copy-done((f32[1,256,256]{2,1,0:T(8,128)S(1)}, f32[1,256,256]{2,1,0:T(8,128)}, u32[]{:S(2)}) %copy-start) | copy-done | bytes 262168
  3.0 0.0 copy-start.1
  3.0 0.9 %copy-done.1 = f32[1,256,256]{2,1,0:T(8,128)S(1)} copy-done((f32[1,256,256]{2,1,0:T(8,128)S(1)}, f32[1,256,256]{2,1,0:T(8,128)}, u32[]{:S(2)}) %copy-start.1) | copy-done | bytes 262168
  3.9 0.0 copy-start.2
  3.9 0.9 %copy-done.2 = f32[1,1,16,32,32]{4,3,2,1,0:T(8,128)S(1)} copy-done((f32[1,1,16,32,32]{4,3,2,1,0:T(8,128)S(1)}, f32[1,1,16,32,32]{4,3,2,1,0:T(8,128)}, u32[]{:S(2)}) %copy-start.2) | copy-done | bytes 65560
  4.9 0.0 copy-start.3
  4.9 0.9 %copy-done.3 = bf16[2,256,256]{2,1,0:T(8,128)(2,1)S(1)} copy-done((bf16[2,256,256]{2,1,0:T(8,128)(2,1)S(1)}, bf16[2,256,256]{2,1,0:T(8,128)(2,1)}, u32[]{:S(2)}) %copy-start.3) | copy-done | bytes 262168
  5.8 0.0 copy-start.4
  5.8 0.9 %copy-done.4 = bf16[2,256,256]{2,1,0:T(8,128)(2,1)S(1)} copy-done((bf16[2,256,256]{2,1,0:T(8,128)(2,1)S(1)}, bf16[2,256,256]{2,1,0:T(8,128)(2,1)}, u32[]{:S(2)}) %copy-start.4) | copy-done | bytes 262168
  6.8 0.0 copy-start.5
  6.8 0.9 %copy-done.5 = bf16[2,192,192]{2,1,0:T(8,128)(2,1)S(1)} copy-done((bf16[2,192,192]{2,1,0:T(8,128)(2,1)S(1)}, bf16[2,192,192]{2,1,0:T(8,128)(2,1)}, u32[]{:S(2)}) %copy-start.5) | copy-done | bytes 147480
  7.7 0.0 copy-start.6
  7.7 0.9 %copy-done.6 = bf16[2,192,192]{2,1,0:T(8,128)(2,1)S(1)} copy-done((bf16[2,192,192]{2,1,0:T(8,128)(2,1)S(1)}, bf16[2,192,192]{2,1,0:T(8,128)(2,1)}, u32[]{:S(2)}) %copy-start.6) | copy-done | bytes 147480
  8.6 0.0 copy-start.7
  8.6 0.8 %copy-done.7 = f32[1,3,32,32]{3,2,1,0:T(8,128)S(1)} copy-done((f32[1,3,32,32]{3,2,1,0:T(8,128)S(1)}, f32[1,3,32,32]{3,2,1,0:T(8,128)}, u32[]{:S(2)}) %copy-start.7) | copy-done | bytes 12312
  9.4 0.0 copy-start.8
  9.4 0.8 %copy-done.8 = f32[1,3,32,32]{3,2,1,0:T(8,128)S(1)} copy-done((f32[1,3,32,32]{3,2,1,0:T(8,128)S(1)}, f32[1,3,32,32]{3,2,1,0:T(8,128)}, u32[]{:S(2)}) %copy-start.8) | copy-done | bytes 12312
  10.2 0.0 copy-start.9
  10.2 2.7 %shard_map.131.fields = f32[2,5,128,256]{3,2,1,0:T(8,128)S(1)} custom-call(s32[16,2]{1,0:T(8,128)S(1)} %copy.14.corners, s32[1,1]{1,0:T(1,128)S(6)} %copy.17.tallies, f32[1,256,256]{2,1,0:T(8,128)S(1)} %copy-done, f32[1,256,256]{2,1,0:T(8,128)S(1)} %copy-done.1, f32[1,3,32,32]{3,2,1,0:T(8,128)S(1)} %copy-done.7, f32[1,3,32,32]{3,2,1,0:T(8,128)S(1)} %copy-done.8, ...), custom_call_target="tpu_custom_call" | custom-call | tf_op jit(solution)/shard_map/pallas_call | solution.py:264
  13.0 0.0 copy-done.9
  13.0 35.6 %shard_map.132 = (f32[2,128,256]{2,1,0:T(8,128)S(1)}, f32[2,16,256]{2,1,0:T(8,128)S(1)}) custom-call(f32[2,5,128,256]{3,2,1,0:T(8,128)S(1)} %shard_map.131.fields, f32[16,128]{1,0:T(8,128)S(1)} %copy-done.9), custom_call_target="tpu_custom_call" | custom-call | tf_op jit(solution)/shard_map/pallas_call | solution.py:285
  48.6 1.0 %copy.15 = f32[2,1,128,1,256]{4,3,2,1,0:T(1,128)} copy(f32[2,1,128,1,256]{4,2,0,3,1:T(8,128)S(1)} %bitcast.2) | data formatting | bytes 524288
  49.5 0.6 %copy.18 = f32[2,16,256]{2,1,0:T(8,128)} copy(f32[2,16,256]{2,1,0:T(8,128)S(1)} %get-tuple-element.11) | data formatting | bytes 65536
Async XLA Ops:
  2.0 0.9 %copy-start = (f32[1,256,256]{2,1,0:T(8,128)S(1)}, f32[1,256,256]{2,1,0:T(8,128)}, u32[]{:S(2)}) copy-start(f32[1,256,256]{2,1,0:T(8,128)} %o_re.1) | copy-start | bytes 786436
  3.0 0.9 %copy-start.1 = (f32[1,256,256]{2,1,0:T(8,128)S(1)}, f32[1,256,256]{2,1,0:T(8,128)}, u32[]{:S(2)}) copy-start(f32[1,256,256]{2,1,0:T(8,128)} %o_im.1) | copy-start | bytes 786436
  3.9 0.9 %copy-start.2 = (f32[1,1,16,32,32]{4,3,2,1,0:T(8,128)S(1)}, f32[1,1,16,32,32]{4,3,2,1,0:T(8,128)}, u32[]{:S(2)}) copy-start(f32[1,1,16,32,32]{4,3,2,1,0:T(8,128)} %intensity.1) | copy-start | bytes 196612
  4.9 0.9 %copy-start.3 = (bf16[2,256,256]{2,1,0:T(8,128)(2,1)S(1)}, bf16[2,256,256]{2,1,0:T(8,128)(2,1)}, u32[]{:S(2)}) copy-start(bf16[2,256,256]{2,1,0:T(8,128)(2,1)} %constant.10.clone.right_b) | copy-start | bytes 786436
  5.8 0.9 %copy-start.4 = (bf16[2,256,256]{2,1,0:T(8,128)(2,1)S(1)}, bf16[2,256,256]{2,1,0:T(8,128)(2,1)}, u32[]{:S(2)}) copy-start(bf16[2,256,256]{2,1,0:T(8,128)(2,1)} %constant.8.clone.right_f) | copy-start | bytes 786436
  6.8 0.9 %copy-start.5 = (bf16[2,192,192]{2,1,0:T(8,128)(2,1)S(1)}, bf16[2,192,192]{2,1,0:T(8,128)(2,1)}, u32[]{:S(2)}) copy-start(bf16[2,192,192]{2,1,0:T(8,128)(2,1)} %constant.11.clone.left_b) | copy-start | bytes 442372
  7.7 0.9 %copy-start.6 = (bf16[2,192,192]{2,1,0:T(8,128)(2,1)S(1)}, bf16[2,192,192]{2,1,0:T(8,128)(2,1)}, u32[]{:S(2)}) copy-start(bf16[2,192,192]{2,1,0:T(8,128)(2,1)} %constant.9.clone.left_f) | copy-start | bytes 442372
  8.6 0.8 %copy-start.7 = (f32[1,3,32,32]{3,2,1,0:T(8,128)S(1)}, f32[1,3,32,32]{3,2,1,0:T(8,128)}, u32[]{:S(2)}) copy-start(f32[1,3,32,32]{3,2,1,0:T(8,128)} %p_re.1) | copy-start | bytes 36868
  9.4 0.8 %copy-start.8 = (f32[1,3,32,32]{3,2,1,0:T(8,128)S(1)}, f32[1,3,32,32]{3,2,1,0:T(8,128)}, u32[]{:S(2)}) copy-start(f32[1,3,32,32]{3,2,1,0:T(8,128)} %p_im.1) | copy-start | bytes 36868
  10.2 2.7 %copy-start.9 = (f32[16,128]{1,0:T(8,128)S(1)}, f32[16,128]{1,0:T(8,128)}, u32[]{:S(2)}) copy-start(f32[16,128]{1,0:T(8,128)} %templates_ref.1) | copy-start | bytes 24580

commit v2 on v1

--- a/solution.py
+++ b/solution.py
@@ -56,28 +56,7 @@
     return dot(a[0], b[0]) + (dot(a[0], b[1]) + dot(a[1], b[0]))
 
 
-def slots_kernel(
-    corners,
-    tallies,
-    o_re,
-    o_im,
-    p_re,
-    p_im,
-    intensity,
-    right_f,
-    left_f,
-    right_b,
-    left_b,
-    out,
-    objects,
-    totals,
-):
-    tally = tallies[0, 0]
-    for part, source in enumerate((o_re, o_im)):
-        for half in range(2):
-            lanes = slice(half * HALF, (half + 1) * HALF)
-            objects[pl.ds(2 * part + half, SIDE, stride=4), :] = source[0, :, lanes]
-    totals[...] = jnp.zeros_like(totals)
+def slot_terms(corners, tally, objects, p_re, p_im, intensity, right_f, left_f, right_b, left_b):
     probe_re = [jnp.concatenate([p_re[0, m]] * PER_GROUP, axis=1) for m in range(MODES)]
     probe_im = [jnp.concatenate([p_im[0, m]] * PER_GROUP, axis=1) for m in range(MODES)]
     light = sum(a * a + b * b for a, b in zip(probe_re, probe_im))
@@ -88,7 +67,7 @@
         patch = [jnp.zeros((WIDTH, LANES), jnp.float32)] * 2
         for j in range(PER_GROUP):
             s = g * PER_GROUP + j
-            row, column = corners[s, 0], corners[s, 1]
+            row, column = corners[0, s], corners[1, s]
             shift = lax.rem(WIDTH * j + SIDE - column, HALF)
             for part in range(2):
                 left, right = (objects[pl.ds(4 * row + 2 * part + half, WIDTH, stride=4), :] for half in range(2))
@@ -126,6 +105,7 @@
         axis=0,
     )
     back = product(halves(wide), (right_b[0], right_b[1]))
+    placed = []
     for g in range(GROUPS):
         term_re, term_im = jnp.zeros((2, WIDTH, LANES), jnp.float32)
         for m in range(MODES):
@@ -135,20 +115,27 @@
             term_im += probe_re[m] * b_im - probe_im[m] * b_re
         for j in range(PER_GROUP):
             s = g * PER_GROUP + j
-            row, column = corners[s, 0], corners[s, 1]
+            column = corners[1, s]
             shift = lax.rem(column + HALF - WIDTH * j, HALF)
             weight = jnp.where(s < tally, 1.0, 0.0)
-            for field, term in enumerate((term_re, term_im, light * weight)):
+            parts = []
+            for term in (term_re, term_im, light * weight):
                 alone = pltpu.roll(jnp.where(lane // WIDTH == j, term, 0.0), shift, 1)
-                for half, part in enumerate((jnp.where(lane >= column, alone, 0.0), jnp.where(lane < column, alone, 0.0))):
-                    totals[field, pl.ds(2 * row + half, WIDTH, stride=2), :] += part
-    for parity in range(2):
-        for half in range(2):
-            lanes = slice(half * HALF, (half + 1) * HALF)
-            for field in range(3):
-                out[parity, field, :, lanes] = totals[field, pl.ds(2 * parity + half, SIDE // 2, stride=4), :]
-            for part in range(2):
-                out[parity, 3 + part, :, lanes] = objects[pl.ds(4 * parity + 2 * part + half, SIDE // 2, stride=8), :]
+                parts += [jnp.where(lane >= column, alone, 0.0), jnp.where(lane < column, alone, 0.0)]
+            placed.append(jnp.concatenate(parts, axis=1))
+    return jnp.concatenate(placed, axis=0)
+
+
+def row_choice(corners, parity):
+    lane = lax.broadcasted_iota(jnp.int32, (HALF, LANES), 1)
+    row = 2 * lax.broadcasted_iota(jnp.int32, (HALF, LANES), 0) + parity
+    choices = []
+    for g in range(GROUPS):
+        first = jnp.zeros((HALF, LANES), jnp.int32)
+        for j in range(PER_GROUP):
+            first = jnp.where(lane // WIDTH == j, corners[0, g * PER_GROUP + j] - WIDTH * j, first)
+        choices.append(jnp.where(row == first + lane, 1.0, 0.0).astype(jnp.bfloat16))
+    return jnp.concatenate(choices, axis=1)
 
 
 def projection(templates):
@@ -165,20 +152,44 @@
     return table[:, ENERGIES:]
 
 
-def exchange_kernel(
-    fields,
-    templates_ref,
-    fitted,
-    coefficients,
-    partner,
-    spectra,
-    values,
-    answer,
-    landed,
-    arrivals,
-    sems,
+def step_kernel(
+    corners,
+    tallies,
+    *refs,
 ):
+    sources, (fitted, coefficients), (
+        o_re,
+        o_im,
+        p_re,
+        p_im,
+        intensity,
+        right_f,
+        left_f,
+        right_b,
+        left_b,
+        templates_ref,
+        objects,
+        away,
+        partner,
+        spectra,
+        values,
+        answer,
+        arrivals,
+        local_sems,
+        sems,
+    ) = refs[:SOURCES], refs[SOURCES : SOURCES + 2], refs[SOURCES + 2 :]
     me, core = lax.axis_index("ea"), lax.axis_index("ta")
+    copies = [
+        pltpu.make_async_copy(source, target, local_sems.at[k])
+        for k, (source, target) in enumerate(
+            zip(
+                sources,
+                (o_re, o_im, p_re, p_im, intensity, right_f, left_f, right_b, left_b, templates_ref),
+            )
+        )
+    ]
+    for copy in copies:
+        copy.start()
     barrier = pltpu.get_barrier_semaphore()
 
     def peer_of(step):
@@ -190,10 +201,25 @@
 
     pl.semaphore_signal(barrier, inc=1, device_id={"ta": 1 - core}, device_id_type=MESH)
     lax.fori_loop(0, ENERGIES - 1, greet, 0)
+    for copy in copies:
+        copy.wait()
+    for part, source in enumerate((o_re, o_im)):
+        for half in range(2):
+            lanes = slice(half * HALF, (half + 1) * HALF)
+            objects[pl.ds(2 * part + half, SIDE, stride=4), :] = source[0, :, lanes]
+    placed = halves(
+        slot_terms(corners, tallies[0, 0], objects, p_re, p_im, intensity, right_f, left_f, right_b, left_b)
+    )
+
+    def summed(parity):
+        choice = row_choice(corners, parity)
+        dot = functools.partial(jnp.dot, preferred_element_type=jnp.float32)
+        return dot(choice, placed[0]) + dot(choice, placed[1])
+
+    away[...] = summed(1 - core)
     pl.semaphore_wait(barrier, ENERGIES)
-
     swap = pltpu.make_async_remote_copy(
-        src_ref=fields.at[1 - core, pl.ds(0, 3)],
+        src_ref=away,
         dst_ref=partner,
         send_sem=sems.at[0],
         recv_sem=sems.at[1],
@@ -201,18 +227,22 @@
         device_id_type=MESH,
     )
     swap.start()
+    here = summed(core)
     swap.wait()
-    scale = fields[core, 2] + partner[2] + REGULARIZER
+    scale = here[:, 2 * SIDE :] + partner[:, 2 * SIDE :] + REGULARIZER
     for part in range(2):
-        own = fields[core, 3 + part]
-        spectra[:, part * SIDE : (part + 1) * SIDE] = own - (fields[core, part] + partner[part]) / scale
-
-    def send_all(source, target, first):
+        lanes = slice(part * SIDE, (part + 1) * SIDE)
+        own = jnp.concatenate(
+            [objects[pl.ds(4 * core + 2 * part + half, HALF, stride=8), :] for half in range(2)], axis=1
+        )
+        spectra[part] = own - (here[:, lanes] + partner[:, lanes]) / scale
+
+    def send_all(source, target, part, first):
         def send(step, carry):
             peer = peer_of(step)
             pltpu.make_async_remote_copy(
-                src_ref=source.at[pl.ds(peer, 1)],
-                dst_ref=target.at[pl.ds(me, 1)],
+                src_ref=source.at[part, pl.ds(peer, 1)],
+                dst_ref=target.at[part, pl.ds(me, 1)],
                 send_sem=sems.at[first],
                 recv_sem=sems.at[first + 1],
                 device_id={"ea": peer},
@@ -221,7 +251,7 @@
             return carry
 
         lax.fori_loop(0, ENERGIES - 1, send, 0)
-        target[pl.ds(me, 1), :] = source[pl.ds(me, 1), :]
+        target[part, pl.ds(me, 1), :] = source[part, pl.ds(me, 1), :]
 
     def wait_all(first):
         pltpu.make_async_remote_copy(
@@ -233,20 +263,23 @@
             device_id_type=MESH,
         ).wait()
 
-    send_all(spectra, values, 2)
+    for part in range(2):
+        send_all(spectra, values, part, 2 + 2 * part)
     templates = templates_ref[...]
     project = projection(templates)
-    wait_all(2)
-    coefs = jnp.dot(project, values[...], precision=HIGHEST, preferred_element_type=jnp.float32)
     for part in range(2):
-        coefficients[part] = coefs[:, part * SIDE : (part + 1) * SIDE]
-    answer[...] = lax.dot_general(
-        templates, coefs, (((0,), (0,)), ((), ())), precision=HIGHEST, preferred_element_type=jnp.float32
-    )
-    send_all(answer, landed, 4)
-    wait_all(4)
+        wait_all(2 + 2 * part)
+        coefs = jnp.dot(project, values[part], precision=HIGHEST, preferred_element_type=jnp.float32)
+        coefficients[part] = coefs
+        answer[part] = lax.dot_general(
+            templates, coefs, (((0,), (0,)), ((), ())), precision=HIGHEST, preferred_element_type=jnp.float32
+        )
+        send_all(answer, fitted, part, 6 + 2 * part)
     for part in range(2):
-        fitted[part] = landed[:, part * SIDE : (part + 1) * SIDE]
+        wait_all(6 + 2 * part)
+
+
+SOURCES = 10
 
 
 def local(
@@ -261,48 +294,40 @@
 ):
     vmem = pl.BlockSpec(memory_space=pltpu.VMEM)
     smem = pl.BlockSpec(memory_space=pltpu.SMEM)
-    fields = pl.pallas_call(
-        slots_kernel,
-        out_shape=jax.ShapeDtypeStruct((2, 5, SIDE // 2, SIDE), jnp.float32),
-        in_specs=[smem, smem] + [vmem] * 9,
-        out_specs=vmem,
-        scratch_shapes=[
-            pltpu.VMEM((4 * SIDE, HALF), jnp.float32),
-            pltpu.VMEM((3, 2 * SIDE, HALF), jnp.float32),
-        ],
-        compiler_params=pltpu.CompilerParams(vmem_limit_bytes=VMEM_BYTES),
-    )(
-        window_corners[0, 0],
-        filled_tallies,
+    sources = (
         sample_inphase,
         sample_quadrature,
         beam_inphase,
         beam_quadrature,
         recorded_diffraction,
         *[jnp.asarray(table) for table in dft_matrices()],
-    )
-    rows = pltpu.VMEM((ENERGIES, 2 * SIDE), jnp.float32)
+        absorption_templates,
+    )
+    rows = pltpu.VMEM((2, ENERGIES, SIDE), jnp.float32)
     fitted, coefficients = pl.pallas_call(
-        exchange_kernel,
+        step_kernel,
         out_shape=(
             jax.ShapeDtypeStruct((2, ENERGIES, SIDE), jnp.float32),
             jax.ShapeDtypeStruct((2, EDGES, SIDE), jnp.float32),
         ),
-        in_specs=[vmem] * 2,
+        in_specs=[smem, smem] + [pl.BlockSpec(memory_space=pl.ANY)] * SOURCES,
         out_specs=(vmem, vmem),
-        scratch_shapes=[
-            pltpu.VMEM((3, SIDE // 2, SIDE), jnp.float32),
+        scratch_shapes=[pltpu.VMEM(source.shape, source.dtype) for source in sources]
+        + [
+            pltpu.VMEM((4 * SIDE, HALF), jnp.float32),
+            pltpu.VMEM((HALF, 3 * SIDE), jnp.float32),
+            pltpu.VMEM((HALF, 3 * SIDE), jnp.float32),
             rows,
             rows,
             rows,
-            rows,
-            pltpu.VMEM((ENERGIES - 1, 1, 2 * SIDE), jnp.float32),
-            pltpu.SemaphoreType.DMA((6,)),
+            pltpu.VMEM((ENERGIES - 1, 1, SIDE), jnp.float32),
+            pltpu.SemaphoreType.DMA((SOURCES,)),
+            pltpu.SemaphoreType.DMA((10,)),
         ],
         compiler_params=pltpu.CompilerParams(
             collective_id=0, has_side_effects=True, vmem_limit_bytes=VMEM_BYTES
         ),
-    )(fields, absorption_templates)
+    )(window_corners[0, 0].T, filled_tallies, *sources)
     return (fitted[:, None, :, None, :], coefficients)
 
 

time: 50.6 us -> 49.2 us (0.972)
  Pallas kernels: 38.3 us -> 36.3 us
  local copies, waits for them, and re-layouts: 10.5 us -> 11.2 us
    pallas_call x2 -> x1, Pallas kernels: 38.3 us -> 36.3 us  [local(): pl.pallas_call(step_kernel, out_shape=(jax.ShapeDtypeStruct((2, ENERGIES,...]
    unnamed x22 -> x24, local copies, waits for them, and re-layouts: 9.79 us -> 11.2 us
    squeeze x1 -> x0, local copies, waits for them, and re-layouts: 0.76 us -> none  [local(): window_corners[0, 0]]
where the time goes in v2:
time: 49.2 us; the launch traced here: 48.7 us
  Pallas kernels  36.3 us (74%)
  local copies, waits for them, and re-layouts  11.2 us (23%)
  between operations  1.31 us (3%)
    pallas_call x1, Pallas kernels, local(): pl.pallas_call(step_kernel, out_shape=(jax.ShapeDtypeStruct((2, ENERGIES,...  36.3 us
    unnamed x24, local copies, waits for them, and re-layouts  11.2 us

profile of v2, /device:TPU:1, one launch (start us, length us, event | category | flops | bytes accessed | tf_op | source)
XLA Modules:
  0.0 48.7 jit_solution(9048071251325037164)
XLA Ops:
  1.3 0.0 copy-start.10
  1.3 0.7 %copy-done.10 = s32[1,1,16,2]{2,3,1,0:T(2,128)S(1)} copy-done((s32[1,1,16,2]{2,3,1,0:T(2,128)S(1)}, s32[1,1,16,2]{2,3,1,0:T(2,128)}, u32[]{:S(2)}) %copy-start.10) | copy-done | bytes 152
  2.0 0.0 copy-start
  2.0 0.9 %copy-done = f32[1,256,256]{2,1,0:T(8,128)S(1)} copy-done((f32[1,256,256]{2,1,0:T(8,128)S(1)}, f32[1,256,256]{2,1,0:T(8,128)}, u32[]{:S(2)}) %copy-start) | copy-done | bytes 262168
  2.9 0.0 copy-start.1
  2.9 0.9 %copy-done.1 = f32[1,256,256]{2,1,0:T(8,128)S(1)} copy-done((f32[1,256,256]{2,1,0:T(8,128)S(1)}, f32[1,256,256]{2,1,0:T(8,128)}, u32[]{:S(2)}) %copy-start.1) | copy-done | bytes 262168
  3.9 0.0 copy-start.2
  3.9 0.9 %copy-done.2 = f32[1,1,16,32,32]{4,3,2,1,0:T(8,128)S(1)} copy-done((f32[1,1,16,32,32]{4,3,2,1,0:T(8,128)S(1)}, f32[1,1,16,32,32]{4,3,2,1,0:T(8,128)}, u32[]{:S(2)}) %copy-start.2) | copy-done | bytes 65560
  4.8 0.0 copy-start.3
  4.8 0.9 %copy-done.3 = bf16[2,256,256]{2,1,0:T(8,128)(2,1)S(1)} copy-done((bf16[2,256,256]{2,1,0:T(8,128)(2,1)S(1)}, bf16[2,256,256]{2,1,0:T(8,128)(2,1)}, u32[]{:S(2)}) %copy-start.3) | copy-done | bytes 262168
  5.8 0.0 copy-start.4
  5.8 0.9 %copy-done.4 = bf16[2,256,256]{2,1,0:T(8,128)(2,1)S(1)} copy-done((bf16[2,256,256]{2,1,0:T(8,128)(2,1)S(1)}, bf16[2,256,256]{2,1,0:T(8,128)(2,1)}, u32[]{:S(2)}) %copy-start.4) | copy-done | bytes 262168
  6.7 0.0 copy-start.5
  6.7 0.9 %copy-done.5 = bf16[2,192,192]{2,1,0:T(8,128)(2,1)S(1)} copy-done((bf16[2,192,192]{2,1,0:T(8,128)(2,1)S(1)}, bf16[2,192,192]{2,1,0:T(8,128)(2,1)}, u32[]{:S(2)}) %copy-start.5) | copy-done | bytes 147480
  7.6 0.0 copy-start.6
  7.6 0.9 %copy-done.6 = bf16[2,192,192]{2,1,0:T(8,128)(2,1)S(1)} copy-done((bf16[2,192,192]{2,1,0:T(8,128)(2,1)S(1)}, bf16[2,192,192]{2,1,0:T(8,128)(2,1)}, u32[]{:S(2)}) %copy-start.6) | copy-done | bytes 147480
  8.6 0.0 copy-start.7
  8.6 0.8 %copy-done.7 = f32[1,3,32,32]{3,2,1,0:T(8,128)S(1)} copy-done((f32[1,3,32,32]{3,2,1,0:T(8,128)S(1)}, f32[1,3,32,32]{3,2,1,0:T(8,128)}, u32[]{:S(2)}) %copy-start.7) | copy-done | bytes 12312
  9.4 0.0 copy-start.8
  9.4 0.8 %copy-done.8 = f32[1,3,32,32]{3,2,1,0:T(8,128)S(1)} copy-done((f32[1,3,32,32]{3,2,1,0:T(8,128)S(1)}, f32[1,3,32,32]{3,2,1,0:T(8,128)}, u32[]{:S(2)}) %copy-start.8) | copy-done | bytes 12312
  10.2 0.0 copy-start.9
  10.2 0.7 %copy-done.9 = f32[16,128]{1,0:T(8,128)S(1)} copy-done((f32[16,128]{1,0:T(8,128)S(1)}, f32[16,128]{1,0:T(8,128)}, u32[]{:S(2)}) %copy-start.9) | copy-done | bytes 8216
  10.9 36.3 %shard_map.131 = (f32[2,128,256]{2,1,0:T(8,128)S(1)}, f32[2,16,256]{2,1,0:T(8,128)S(1)}) custom-call(s32[2,16]{1,0:T(2,128)S(1)} %bitcast.5, s32[1,1]{1,0:T(1,128)S(6)} %copy.16.tallies, f32[1,256,256]{2,1,0:T(8,128)S(1)} %copy-done, f32[1,256,256]{2,1,0:T(8,128)S(1)} %copy-done.1, f32[1,3,32,32]{3,2,1,0:T(8,128)S(1)} %copy-done.7, ...), custom_call_target="tpu_custom_call" | custom-call | tf_op jit(solution)/shard_map/pallas_call | solution.py:307
  47.1 1.0 %copy.14 = f32[2,1,128,1,256]{4,3,2,1,0:T(1,128)} copy(f32[2,1,128,1,256]{4,2,0,3,1:T(8,128)S(1)} %bitcast.4) | data formatting | bytes 524288
  48.1 0.6 %copy.17 = f32[2,16,256]{2,1,0:T(8,128)} copy(f32[2,16,256]{2,1,0:T(8,128)S(1)} %get-tuple-element.11) | data formatting | bytes 65536
Async XLA Ops:
  1.3 0.7 %copy-start.10 = (s32[1,1,16,2]{2,3,1,0:T(2,128)S(1)}, s32[1,1,16,2]{2,3,1,0:T(2,128)}, u32[]{:S(2)}) copy-start(s32[1,1,16,2]{2,3,1,0:T(2,128)} %param.17) | copy-start | bytes 388
  2.0 0.9 %copy-start = (f32[1,256,256]{2,1,0:T(8,128)S(1)}, f32[1,256,256]{2,1,0:T(8,128)}, u32[]{:S(2)}) copy-start(f32[1,256,256]{2,1,0:T(8,128)} %refs_0_.1) | copy-start | bytes 786436
  2.9 0.9 %copy-start.1 = (f32[1,256,256]{2,1,0:T(8,128)S(1)}, f32[1,256,256]{2,1,0:T(8,128)}, u32[]{:S(2)}) copy-start(f32[1,256,256]{2,1,0:T(8,128)} %refs_1_.1) | copy-start | bytes 786436
  3.9 0.9 %copy-start.2 = (f32[1,1,16,32,32]{4,3,2,1,0:T(8,128)S(1)}, f32[1,1,16,32,32]{4,3,2,1,0:T(8,128)}, u32[]{:S(2)}) copy-start(f32[1,1,16,32,32]{4,3,2,1,0:T(8,128)} %refs_4_.1) | copy-start | bytes 196612
  4.8 0.9 %copy-start.3 = (bf16[2,256,256]{2,1,0:T(8,128)(2,1)S(1)}, bf16[2,256,256]{2,1,0:T(8,128)(2,1)}, u32[]{:S(2)}) copy-start(bf16[2,256,256]{2,1,0:T(8,128)(2,1)} %constant.10.clone.refs_7_) | copy-start | bytes 786436
  5.8 0.9 %copy-start.4 = (bf16[2,256,256]{2,1,0:T(8,128)(2,1)S(1)}, bf16[2,256,256]{2,1,0:T(8,128)(2,1)}, u32[]{:S(2)}) copy-start(bf16[2,256,256]{2,1,0:T(8,128)(2,1)} %constant.8.clone.refs_5_) | copy-start | bytes 786436
  6.7 0.9 %copy-start.5 = (bf16[2,192,192]{2,1,0:T(8,128)(2,1)S(1)}, bf16[2,192,192]{2,1,0:T(8,128)(2,1)}, u32[]{:S(2)}) copy-start(bf16[2,192,192]{2,1,0:T(8,128)(2,1)} %constant.11.clone.refs_8_) | copy-start | bytes 442372
  7.6 0.9 %copy-start.6 = (bf16[2,192,192]{2,1,0:T(8,128)(2,1)S(1)}, bf16[2,192,192]{2,1,0:T(8,128)(2,1)}, u32[]{:S(2)}) copy-start(bf16[2,192,192]{2,1,0:T(8,128)(2,1)} %constant.9.clone.refs_6_) | copy-start | bytes 442372
  8.6 0.8 %copy-start.7 = (f32[1,3,32,32]{3,2,1,0:T(8,128)S(1)}, f32[1,3,32,32]{3,2,1,0:T(8,128)}, u32[]{:S(2)}) copy-start(f32[1,3,32,32]{3,2,1,0:T(8,128)} %refs_2_.1) | copy-start | bytes 36868
  9.4 0.8 %copy-start.8 = (f32[1,3,32,32]{3,2,1,0:T(8,128)S(1)}, f32[1,3,32,32]{3,2,1,0:T(8,128)}, u32[]{:S(2)}) copy-start(f32[1,3,32,32]{3,2,1,0:T(8,128)} %refs_3_.1) | copy-start | bytes 36868
  10.2 0.7 %copy-start.9 = (f32[16,128]{1,0:T(8,128)S(1)}, f32[16,128]{1,0:T(8,128)}, u32[]{:S(2)}) copy-start(f32[16,128]{1,0:T(8,128)} %refs_9_.1) | copy-start | bytes 24580

commit v3 on v2

--- a/solution.py
+++ b/solution.py
@@ -23,7 +23,7 @@
 GROUPS = SLOTS // PER_GROUP
 BAND = MODES * WIDTH
 LANES = PER_GROUP * WIDTH
-VMEM_BYTES = 48 * 1024 * 1024
+VMEM_BYTES = 54 * 1024 * 1024
 
 
 def split_table(table):
@@ -237,21 +237,39 @@
         )
         spectra[part] = own - (here[:, lanes] + partner[:, lanes]) / scale
 
+    x, y, depth = lax.rem(me, 4), me // 32, lax.rem(me // 4, 8)
+    place = (y * 4 + lax.rem(depth, 4)) * 4 + x
+
+    def send_one(source, target, part, first, peer):
+        pltpu.make_async_remote_copy(
+            src_ref=source.at[part, pl.ds(peer, 1)],
+            dst_ref=target.at[part, pl.ds(me, 1)],
+            send_sem=sems.at[first],
+            recv_sem=sems.at[first + 1],
+            device_id={"ea": peer},
+            device_id_type=MESH,
+        ).start()
+
     def send_all(source, target, part, first):
         def send(step, carry):
-            peer = peer_of(step)
-            pltpu.make_async_remote_copy(
-                src_ref=source.at[part, pl.ds(peer, 1)],
-                dst_ref=target.at[part, pl.ds(me, 1)],
-                send_sem=sems.at[first],
-                recv_sem=sems.at[first + 1],
-                device_id={"ea": peer},
-                device_id_type=MESH,
-            ).start()
+            send_one(source, target, part, first, peer_of(step))
             return carry
 
-        lax.fori_loop(0, ENERGIES - 1, send, 0)
+        lax.fori_loop(0, ENERGIES - 1, send, 0, unroll=8)
         target[part, pl.ds(me, 1), :] = source[part, pl.ds(me, 1), :]
+
+    def send_side(source, target, part, first, side):
+        def send(step, carry):
+            spot = lax.rem(place + step, 64)
+            peer = (spot // 16) * 32 + side * 16 + lax.rem(spot, 16)
+            send_one(source, target, part, first, peer)
+            return carry
+
+        if side == 0:
+            across = (y * 8 + lax.rem(depth + 4, 8)) * 4 + x
+            send_one(source, target, part, first, across)
+            target[part, pl.ds(me, 1), :] = source[part, pl.ds(me, 1), :]
+        lax.fori_loop(1, 64, send, 0, unroll=9)
 
     def wait_all(first):
         pltpu.make_async_remote_copy(
@@ -267,14 +285,17 @@
         send_all(spectra, values, part, 2 + 2 * part)
     templates = templates_ref[...]
     project = projection(templates)
+    rebuild = lax.dot_general(
+        templates, project, (((0,), (0,)), ((), ())), precision=HIGHEST, preferred_element_type=jnp.float32
+    )
+    solve = jnp.concatenate([rebuild, project], axis=0)
     for part in range(2):
         wait_all(2 + 2 * part)
-        coefs = jnp.dot(project, values[part], precision=HIGHEST, preferred_element_type=jnp.float32)
-        coefficients[part] = coefs
-        answer[part] = lax.dot_general(
-            templates, coefs, (((0,), (0,)), ((), ())), precision=HIGHEST, preferred_element_type=jnp.float32
-        )
-        send_all(answer, fitted, part, 6 + 2 * part)
+        both = jnp.dot(solve, values[part], precision=HIGHEST, preferred_element_type=jnp.float32)
+        answer[part] = both[:ENERGIES]
+        coefficients[part] = both[ENERGIES:]
+        for side in range(2):
+            send_side(answer, fitted, part, 6 + 2 * part, side)
     for part in range(2):
         wait_all(6 + 2 * part)
 

time: 49.2 us -> 39.1 us (0.79)
  local copies, waits for them, and re-layouts: 11.2 us -> 2.55 us
  Pallas kernels: 36.3 us -> 35.1 us
    unnamed x24 -> x4, local copies, waits for them, and re-layouts: 11.2 us -> 2.55 us
    pallas_call x1, Pallas kernels: 36.3 us -> 35.1 us  [local(): pl.pallas_call(step_kernel, out_shape=(jax.ShapeDtypeStruct((2, ENERGIES,...]
where the time goes in v3:
time: 39.1 us; the launch traced here: 39 us
  Pallas kernels  35.1 us (90%)
  local copies, waits for them, and re-layouts  2.55 us (7%)
  between operations  1.3 us (3%)
    pallas_call x1, Pallas kernels, local(): pl.pallas_call(step_kernel, out_shape=(jax.ShapeDtypeStruct((2, ENERGIES,...  35.1 us
    unnamed x4, local copies, waits for them, and re-layouts  2.55 us

profile of v3, /device:TPU:1, one launch (start us, length us, event | category | flops | bytes accessed | tf_op | source)
XLA Modules:
  0.0 39.0 jit_solution(6952454927138119458)
XLA Ops:
  1.3 35.1 %shard_map.131 = (f32[2,128,256]{2,1,0:T(8,128)}, f32[2,16,256]{2,1,0:T(8,128)}) custom-call(s32[2,16]{1,0:T(2,128)} %bitcast.5, s32[1,1]{1,0:T(1,128)S(6)} %copy.16.tallies, f32[1,256,256]{2,1,0:T(8,128)} %refs_0_.1, f32[1,256,256]{2,1,0:T(8,128)} %refs_1_.1, f32[1,3,32,32]{3,2,1,0:T(8,128)} %refs_2_.1, f32[1,3,32,32]{3,2,1,0:T(8,128)} %refs_3_.1, ...), custom_call_target="tpu_custom_call" | custom-call | tf_op jit(solution)/shard_map/pallas_call | solution.py:328
  36.4 0.0 copy-start
  36.4 1.9 %copy.14 = f32[2,1,128,1,256]{4,3,2,1,0:T(1,128)} copy(f32[2,1,128,1,256]{4,2,0,3,1:T(8,128)} %bitcast.4) | data formatting | bytes 524288
  38.4 0.0 copy-done
  38.4 0.6 %copy.17 = f32[2,16,256]{2,1,0:T(8,128)} copy(f32[2,16,256]{2,1,0:T(8,128)S(1)} %copy-done) | data formatting | bytes 65536
Async XLA Ops:
  36.4 1.9 %copy-start = (f32[2,16,256]{2,1,0:T(8,128)S(1)}, f32[2,16,256]{2,1,0:T(8,128)}, u32[]{:S(2)}) copy-start(f32[2,16,256]{2,1,0:T(8,128)} %get-tuple-element.11) | copy-start | bytes 98308

commit v4 on v3

--- a/solution.py
+++ b/solution.py
@@ -119,7 +119,7 @@
             shift = lax.rem(column + HALF - WIDTH * j, HALF)
             weight = jnp.where(s < tally, 1.0, 0.0)
             parts = []
-            for term in (term_re, term_im, light * weight):
+            for term in (term_re, light * weight, term_im):
                 alone = pltpu.roll(jnp.where(lane // WIDTH == j, term, 0.0), shift, 1)
                 parts += [jnp.where(lane >= column, alone, 0.0), jnp.where(lane < column, alone, 0.0)]
             placed.append(jnp.concatenate(parts, axis=1))
@@ -200,7 +200,7 @@
         return carry
 
     pl.semaphore_signal(barrier, inc=1, device_id={"ta": 1 - core}, device_id_type=MESH)
-    lax.fori_loop(0, ENERGIES - 1, greet, 0)
+    lax.fori_loop(0, ENERGIES - 1, greet, 0, unroll=8)
     for copy in copies:
         copy.wait()
     for part, source in enumerate((o_re, o_im)):
@@ -211,39 +211,47 @@
         slot_terms(corners, tallies[0, 0], objects, p_re, p_im, intensity, right_f, left_f, right_b, left_b)
     )
 
-    def summed(parity):
-        choice = row_choice(corners, parity)
+    def summed(choice, columns):
         dot = functools.partial(jnp.dot, preferred_element_type=jnp.float32)
-        return dot(choice, placed[0]) + dot(choice, placed[1])
-
-    away[...] = summed(1 - core)
+        return dot(choice, placed[0][:, columns]) + dot(choice, placed[1][:, columns])
+
+    def swap(lanes, first):
+        return pltpu.make_async_remote_copy(
+            src_ref=away.at[:, lanes],
+            dst_ref=partner.at[:, lanes],
+            send_sem=sems.at[first],
+            recv_sem=sems.at[first + 1],
+            device_id={"ta": 1 - core},
+            device_id_type=MESH,
+        )
+
+    choice = row_choice(corners, 1 - core)
+    firsts, seconds = slice(0, 2 * SIDE), slice(2 * SIDE, 3 * SIDE)
+    swaps = [swap(pl.ds(0, 2 * SIDE), 0), swap(pl.ds(2 * SIDE, SIDE), 12)]
+    away[:, firsts] = summed(choice, firsts)
     pl.semaphore_wait(barrier, ENERGIES)
-    swap = pltpu.make_async_remote_copy(
-        src_ref=away,
-        dst_ref=partner,
-        send_sem=sems.at[0],
-        recv_sem=sems.at[1],
-        device_id={"ta": 1 - core},
-        device_id_type=MESH,
-    )
-    swap.start()
-    here = summed(core)
-    swap.wait()
-    scale = here[:, 2 * SIDE :] + partner[:, 2 * SIDE :] + REGULARIZER
-    for part in range(2):
-        lanes = slice(part * SIDE, (part + 1) * SIDE)
+    swaps[0].start()
+    away[:, seconds] = summed(choice, seconds)
+    swaps[1].start()
+    choice = row_choice(corners, core)
+    here = [summed(choice, firsts), summed(choice, seconds)]
+
+    def update(part, total, scale):
         own = jnp.concatenate(
             [objects[pl.ds(4 * core + 2 * part + half, HALF, stride=8), :] for half in range(2)], axis=1
         )
-        spectra[part] = own - (here[:, lanes] + partner[:, lanes]) / scale
+        spectra[part] = own - total / scale
 
     x, y, depth = lax.rem(me, 4), me // 32, lax.rem(me // 4, 8)
     place = (y * 4 + lax.rem(depth, 4)) * 4 + x
+
+    def landing(target, part):
+        return target.at[part, pl.ds(me, 1)] if target is values else target.at[part, 0, me]
 
     def send_one(source, target, part, first, peer):
         pltpu.make_async_remote_copy(
             src_ref=source.at[part, pl.ds(peer, 1)],
-            dst_ref=target.at[part, pl.ds(me, 1)],
+            dst_ref=landing(target, part),
             send_sem=sems.at[first],
             recv_sem=sems.at[first + 1],
             device_id={"ea": peer},
@@ -257,6 +265,9 @@
 
         lax.fori_loop(0, ENERGIES - 1, send, 0, unroll=8)
         target[part, pl.ds(me, 1), :] = source[part, pl.ds(me, 1), :]
+
+    def keep(part):
+        return pltpu.make_async_copy(answer.at[part, pl.ds(me, 1)], fitted.at[part, 0, me], sems.at[10 + part])
 
     def send_side(source, target, part, first, side):
         def send(step, carry):
@@ -268,7 +279,7 @@
         if side == 0:
             across = (y * 8 + lax.rem(depth + 4, 8)) * 4 + x
             send_one(source, target, part, first, across)
-            target[part, pl.ds(me, 1), :] = source[part, pl.ds(me, 1), :]
+            keep(part).start()
         lax.fori_loop(1, 64, send, 0, unroll=9)
 
     def wait_all(first):
@@ -281,8 +292,13 @@
             device_id_type=MESH,
         ).wait()
 
-    for part in range(2):
-        send_all(spectra, values, part, 2 + 2 * part)
+    swaps[0].wait()
+    scale = here[0][:, SIDE:] + partner[:, SIDE : 2 * SIDE] + REGULARIZER
+    update(0, here[0][:, :SIDE] + partner[:, :SIDE], scale)
+    send_all(spectra, values, 0, 2)
+    swaps[1].wait()
+    update(1, here[1] + partner[:, seconds], scale)
+    send_all(spectra, values, 1, 4)
     templates = templates_ref[...]
     project = projection(templates)
     rebuild = lax.dot_general(
@@ -298,9 +314,25 @@
             send_side(answer, fitted, part, 6 + 2 * part, side)
     for part in range(2):
         wait_all(6 + 2 * part)
+        keep(part).wait()
 
 
 SOURCES = 10
+
+
+def hand_on(fitted, coefficients, fitted_out, coefficients_out, fitted_held, coefficients_held, sems):
+    stages = [
+        (fitted.at[part], fitted_held.at[part], fitted_out.at[part]) for part in range(2)
+    ] + [(coefficients, coefficients_held, coefficients_out)]
+    into = [pltpu.make_async_copy(a, b, sems.at[0, k]) for k, (a, b, c) in enumerate(stages)]
+    onward = [pltpu.make_async_copy(b, c, sems.at[1, k]) for k, (a, b, c) in enumerate(stages)]
+    for copy in into:
+        copy.start()
+    for first, second in zip(into, onward):
+        first.wait()
+        second.start()
+    for copy in onward:
+        copy.wait()
 
 
 def local(
@@ -328,11 +360,11 @@
     fitted, coefficients = pl.pallas_call(
         step_kernel,
         out_shape=(
-            jax.ShapeDtypeStruct((2, ENERGIES, SIDE), jnp.float32),
+            jax.ShapeDtypeStruct((2, 1, ENERGIES, 1, SIDE), jnp.float32),
             jax.ShapeDtypeStruct((2, EDGES, SIDE), jnp.float32),
         ),
         in_specs=[smem, smem] + [pl.BlockSpec(memory_space=pl.ANY)] * SOURCES,
-        out_specs=(vmem, vmem),
+        out_specs=(pl.BlockSpec(memory_space=pl.ANY), vmem),
         scratch_shapes=[pltpu.VMEM(source.shape, source.dtype) for source in sources]
         + [
             pltpu.VMEM((4 * SIDE, HALF), jnp.float32),
@@ -343,13 +375,28 @@
             rows,
             pltpu.VMEM((ENERGIES - 1, 1, SIDE), jnp.float32),
             pltpu.SemaphoreType.DMA((SOURCES,)),
-            pltpu.SemaphoreType.DMA((10,)),
+            pltpu.SemaphoreType.DMA((14,)),
         ],
         compiler_params=pltpu.CompilerParams(
             collective_id=0, has_side_effects=True, vmem_limit_bytes=VMEM_BYTES
         ),
     )(window_corners[0, 0].T, filled_tallies, *sources)
-    return (fitted[:, None, :, None, :], coefficients)
+    whole = pl.BlockSpec(memory_space=pl.ANY)
+    return pl.pallas_call(
+        hand_on,
+        out_shape=(
+            jax.ShapeDtypeStruct(fitted.shape, jnp.float32),
+            jax.ShapeDtypeStruct(coefficients.shape, jnp.float32),
+        ),
+        in_specs=[whole, whole],
+        out_specs=(whole, whole),
+        scratch_shapes=[
+            pltpu.VMEM(fitted.shape, jnp.float32),
+            pltpu.VMEM(coefficients.shape, jnp.float32),
+            pltpu.SemaphoreType.DMA((2, 3)),
+        ],
+        compiler_params=pltpu.CompilerParams(vmem_limit_bytes=VMEM_BYTES),
+    )(fitted, coefficients)
 
 
 def solution(mesh):

time: 39.1 us -> 38.2 us (0.977)
  local copies, waits for them, and re-layouts: 2.55 us -> 0 us
  Pallas kernels: 35.1 us -> 36.7 us
    unnamed x4 -> x0, local copies, waits for them, and re-layouts: 2.55 us -> none
    pallas_call x1 -> x2, Pallas kernels: 35.1 us -> 36.7 us  [the longest x1 35.1 us: local(): pl.pallas_call(step_kernel, out_shape=(jax.ShapeDtypeStruct((2, 1, ENERGI...]
where the time goes in v4:
time: 38.2 us; the launch traced here: 38 us
  Pallas kernels  36.7 us (96%)
  between operations  1.29 us (3%)
    pallas_call x1, Pallas kernels, local(): pl.pallas_call(step_kernel, out_shape=(jax.ShapeDtypeStruct((2, 1, ENERGI...  35.1 us
    pallas_call x1, Pallas kernels, local(): pl.pallas_call(hand_on, out_shape=(jax.ShapeDtypeStruct(fitted.shape, jnp...  1.68 us

profile of v4, /device:TPU:1, one launch (start us, length us, event | category | flops | bytes accessed | tf_op | source)
XLA Modules:
  0.0 38.0 jit_solution(1036109082301677899)
XLA Ops:
  1.3 35.1 %shard_map.131 = (f32[2,1,128,1,256]{4,3,2,1,0:T(1,128)}, f32[2,16,256]{2,1,0:T(8,128)}) custom-call(s32[2,16]{1,0:T(2,128)} %bitcast.3, s32[1,1]{1,0:T(1,128)S(6)} %copy.14.tallies, f32[1,256,256]{2,1,0:T(8,128)} %refs_0_.1, f32[1,256,256]{2,1,0:T(8,128)} %refs_1_.1, f32[1,3,32,32]{3,2,1,0:T(8,128)} %refs_2_.1, f32[1,3,32,32]{3,2,1,0:T(8,128)} %refs_3_.1, ...), custom_call_target="tpu_custom_call" | custom-call | tf_op jit(solution)/shard_map/pallas_call | solution.py:360
  36.4 1.7 %shard_map.132 = (f32[2,1,128,1,256]{4,3,2,1,0:T(1,128)}, f32[2,16,256]{2,1,0:T(8,128)}) custom-call(f32[2,1,128,1,256]{4,3,2,1,0:T(1,128)} %get-tuple-element.4.fitted, f32[2,16,256]{2,1,0:T(8,128)} %get-tuple-element.5.coefficients), custom_call_target="tpu_custom_call" | custom-call | tf_op jit(solution)/shard_map/pallas_call | solution.py:385

commit v5 on v4

--- a/solution.py
+++ b/solution.py
@@ -152,12 +152,10 @@
     return table[:, ENERGIES:]
 
 
-def step_kernel(
-    corners,
-    tallies,
-    *refs,
-):
+def step_kernel(*refs):
     sources, (fitted, coefficients), (
+        corners,
+        tallies,
         o_re,
         o_im,
         p_re,
@@ -184,7 +182,7 @@
         for k, (source, target) in enumerate(
             zip(
                 sources,
-                (o_re, o_im, p_re, p_im, intensity, right_f, left_f, right_b, left_b, templates_ref),
+                (corners, tallies, o_re, o_im, p_re, p_im, intensity, right_f, left_f, right_b, left_b, templates_ref),
             )
         )
     ]
@@ -317,7 +315,7 @@
         keep(part).wait()
 
 
-SOURCES = 10
+SOURCES = 12
 
 
 def hand_on(fitted, coefficients, fitted_out, coefficients_out, fitted_held, coefficients_held, sems):
@@ -346,8 +344,9 @@
     absorption_templates,
 ):
     vmem = pl.BlockSpec(memory_space=pltpu.VMEM)
-    smem = pl.BlockSpec(memory_space=pltpu.SMEM)
     sources = (
+        window_corners[0, 0].T,
+        filled_tallies,
         sample_inphase,
         sample_quadrature,
         beam_inphase,
@@ -363,9 +362,10 @@
             jax.ShapeDtypeStruct((2, 1, ENERGIES, 1, SIDE), jnp.float32),
             jax.ShapeDtypeStruct((2, EDGES, SIDE), jnp.float32),
         ),
-        in_specs=[smem, smem] + [pl.BlockSpec(memory_space=pl.ANY)] * SOURCES,
+        in_specs=[pl.BlockSpec(memory_space=pl.ANY)] * SOURCES,
         out_specs=(pl.BlockSpec(memory_space=pl.ANY), vmem),
-        scratch_shapes=[pltpu.VMEM(source.shape, source.dtype) for source in sources]
+        scratch_shapes=[pltpu.SMEM(source.shape, source.dtype) for source in sources[:2]]
+        + [pltpu.VMEM(source.shape, source.dtype) for source in sources[2:]]
         + [
             pltpu.VMEM((4 * SIDE, HALF), jnp.float32),
             pltpu.VMEM((HALF, 3 * SIDE), jnp.float32),
@@ -380,7 +380,7 @@
         compiler_params=pltpu.CompilerParams(
             collective_id=0, has_side_effects=True, vmem_limit_bytes=VMEM_BYTES
         ),
-    )(window_corners[0, 0].T, filled_tallies, *sources)
+    )(*sources)
     whole = pl.BlockSpec(memory_space=pl.ANY)
     return pl.pallas_call(
         hand_on,

time: 38.2 us -> 37.5 us (0.982)
  Pallas kernels: 36.7 us -> 36.1 us
    pallas_call x1, Pallas kernels: 35.1 us -> 34.4 us  [local(): pl.pallas_call(step_kernel, out_shape=(jax.ShapeDtypeStruct((2, 1, ENERGI...]
where the time goes in v5:
time: 37.5 us; the launch traced here: 37.4 us
  Pallas kernels  36.1 us (96%)
  between operations  1.29 us (3%)
    pallas_call x1, Pallas kernels, local(): pl.pallas_call(step_kernel, out_shape=(jax.ShapeDtypeStruct((2, 1, ENERGI...  34.4 us
    pallas_call x1, Pallas kernels, local(): pl.pallas_call(hand_on, out_shape=(jax.ShapeDtypeStruct(fitted.shape, jnp...  1.68 us

profile of v5, /device:TPU:1, one launch (start us, length us, event | category | flops | bytes accessed | tf_op | source)
XLA Modules:
  0.0 37.4 jit_solution(18326081035157098394)
XLA Ops:
  1.3 34.4 %shard_map.131 = (f32[2,1,128,1,256]{4,3,2,1,0:T(1,128)}, f32[2,16,256]{2,1,0:T(8,128)}) custom-call(s32[2,16]{1,0:T(2,128)} %bitcast.3, s32[1,1]{1,0:T(1,128)S(6)} %copy.14.refs_1_, f32[1,256,256]{2,1,0:T(8,128)} %refs_2_.1, f32[1,256,256]{2,1,0:T(8,128)} %refs_3_.1, f32[1,3,32,32]{3,2,1,0:T(8,128)} %refs_4_.1, f32[1,3,32,32]{3,2,1,0:T(8,128)} %refs_5_.1, ...), custom_call_target="tpu_custom_call" | custom-call | tf_op jit(solution)/shard_map/pallas_call | solution.py:359
  35.7 1.7 %shard_map.132 = (f32[2,1,128,1,256]{4,3,2,1,0:T(1,128)}, f32[2,16,256]{2,1,0:T(8,128)}) custom-call(f32[2,1,128,1,256]{4,3,2,1,0:T(1,128)} %get-tuple-element.4.fitted, f32[2,16,256]{2,1,0:T(8,128)} %get-tuple-element.5.coefficients), custom_call_target="tpu_custom_call" | custom-call | tf_op jit(solution)/shard_map/pallas_call | solution.py:385

commit v6 on v5

--- a/solution.py
+++ b/solution.py
@@ -299,17 +299,19 @@
     send_all(spectra, values, 1, 4)
     templates = templates_ref[...]
     project = projection(templates)
-    rebuild = lax.dot_general(
-        templates, project, (((0,), (0,)), ((), ())), precision=HIGHEST, preferred_element_type=jnp.float32
-    )
-    solve = jnp.concatenate([rebuild, project], axis=0)
+    rebuild = halves(
+        lax.dot_general(
+            templates, project, (((0,), (0,)), ((), ())), precision=HIGHEST, preferred_element_type=jnp.float32
+        )
+    )
     for part in range(2):
         wait_all(2 + 2 * part)
-        both = jnp.dot(solve, values[part], precision=HIGHEST, preferred_element_type=jnp.float32)
-        answer[part] = both[:ENERGIES]
-        coefficients[part] = both[ENERGIES:]
+        answer[part] = product(rebuild, halves(values[part]))
         for side in range(2):
             send_side(answer, fitted, part, 6 + 2 * part, side)
+        coefficients[part] = jnp.dot(
+            project, values[part], precision=HIGHEST, preferred_element_type=jnp.float32
+        )
     for part in range(2):
         wait_all(6 + 2 * part)
         keep(part).wait()

time: 37.5 us -> 37.3 us (level)
  no operation moved by 1% of the time
where the time goes in v6:
time: 37.3 us; the launch traced here: 37.2 us
  Pallas kernels  35.9 us (96%)
  between operations  1.29 us (3%)
    pallas_call x1, Pallas kernels, local(): pl.pallas_call(step_kernel, out_shape=(jax.ShapeDtypeStruct((2, 1, ENERGI...  34.3 us
    pallas_call x1, Pallas kernels, local(): pl.pallas_call(hand_on, out_shape=(jax.ShapeDtypeStruct(fitted.shape, jnp...  1.68 us

profile of v6, /device:TPU:1, one launch (start us, length us, event | category | flops | bytes accessed | tf_op | source)
XLA Modules:
  0.0 37.2 jit_solution(6143446181273442856)
XLA Ops:
  1.3 34.3 %shard_map.131 = (f32[2,1,128,1,256]{4,3,2,1,0:T(1,128)}, f32[2,16,256]{2,1,0:T(8,128)}) custom-call(s32[2,16]{1,0:T(2,128)} %bitcast.3, s32[1,1]{1,0:T(1,128)S(6)} %copy.14.refs_1_, f32[1,256,256]{2,1,0:T(8,128)} %refs_2_.1, f32[1,256,256]{2,1,0:T(8,128)} %refs_3_.1, f32[1,3,32,32]{3,2,1,0:T(8,128)} %refs_4_.1, f32[1,3,32,32]{3,2,1,0:T(8,128)} %refs_5_.1, ...), custom_call_target="tpu_custom_call" | custom-call | tf_op jit(solution)/shard_map/pallas_call | solution.py:361
  35.6 1.7 %shard_map.132 = (f32[2,1,128,1,256]{4,3,2,1,0:T(1,128)}, f32[2,16,256]{2,1,0:T(8,128)}) custom-call(f32[2,1,128,1,256]{4,3,2,1,0:T(1,128)} %get-tuple-element.4.fitted, f32[2,16,256]{2,1,0:T(8,128)} %get-tuple-element.5.coefficients), custom_call_target="tpu_custom_call" | custom-call | tf_op jit(solution)/shard_map/pallas_call | solution.py:387

commit v7 on v5

--- a/solution.py
+++ b/solution.py
@@ -320,7 +320,9 @@
 
 def hand_on(fitted, coefficients, fitted_out, coefficients_out, fitted_held, coefficients_held, sems):
     stages = [
-        (fitted.at[part], fitted_held.at[part], fitted_out.at[part]) for part in range(2)
+        tuple(ref.at[part, :, pl.ds(first, 64)] for ref in (fitted, fitted_held, fitted_out))
+        for part in range(2)
+        for first in range(0, ENERGIES, 64)
     ] + [(coefficients, coefficients_held, coefficients_out)]
     into = [pltpu.make_async_copy(a, b, sems.at[0, k]) for k, (a, b, c) in enumerate(stages)]
     onward = [pltpu.make_async_copy(b, c, sems.at[1, k]) for k, (a, b, c) in enumerate(stages)]
@@ -393,7 +395,7 @@
         scratch_shapes=[
             pltpu.VMEM(fitted.shape, jnp.float32),
             pltpu.VMEM(coefficients.shape, jnp.float32),
-            pltpu.SemaphoreType.DMA((2, 3)),
+            pltpu.SemaphoreType.DMA((2, 5)),
         ],
         compiler_params=pltpu.CompilerParams(vmem_limit_bytes=VMEM_BYTES),
     )(fitted, coefficients)

time: 37.5 us -> 37.5 us (level)
  no operation moved by 1% of the time
where the time goes in v7:
time: 37.5 us; the launch traced here: 37.3 us
  Pallas kernels  36.1 us (96%)
  between operations  1.29 us (3%)
    pallas_call x1, Pallas kernels, local(): pl.pallas_call(step_kernel, out_shape=(jax.ShapeDtypeStruct((2, 1, ENERGI...  34.4 us
    pallas_call x1, Pallas kernels, local(): pl.pallas_call(hand_on, out_shape=(jax.ShapeDtypeStruct(fitted.shape, jnp...  1.66 us

profile of v7, /device:TPU:1, one launch (start us, length us, event | category | flops | bytes accessed | tf_op | source)
XLA Modules:
  0.0 37.3 jit_solution(14980048150215061366)
XLA Ops:
  1.3 34.4 %shard_map.131 = (f32[2,1,128,1,256]{4,3,2,1,0:T(1,128)}, f32[2,16,256]{2,1,0:T(8,128)}) custom-call(s32[2,16]{1,0:T(2,128)} %bitcast.3, s32[1,1]{1,0:T(1,128)S(6)} %copy.14.refs_1_, f32[1,256,256]{2,1,0:T(8,128)} %refs_2_.1, f32[1,256,256]{2,1,0:T(8,128)} %refs_3_.1, f32[1,3,32,32]{3,2,1,0:T(8,128)} %refs_4_.1, f32[1,3,32,32]{3,2,1,0:T(8,128)} %refs_5_.1, ...), custom_call_target="tpu_custom_call" | custom-call | tf_op jit(solution)/shard_map/pallas_call | solution.py:361
  35.7 1.7 %shard_map.132 = (f32[2,1,128,1,256]{4,3,2,1,0:T(1,128)}, f32[2,16,256]{2,1,0:T(8,128)}) custom-call(f32[2,1,128,1,256]{4,3,2,1,0:T(1,128)} %get-tuple-element.4.fitted, f32[2,16,256]{2,1,0:T(8,128)} %get-tuple-element.5.coefficients), custom_call_target="tpu_custom_call" | custom-call | tf_op jit(solution)/shard_map/pallas_call | solution.py:387
